TPU v7x, 32 devices: a whole 2x2x4 slice. The times are simulated.
32 devices in a mesh: groups: 1, pairs: 4 (over z), chol: 4 (over y, x), walk: 2 (over core).
Axes of the slice: x: 2, y: 2, z: 4, core: 2. Of those that a mesh axis runs over, the one named last changes fastest.
Arguments:
- chol_vectors: bfloat16 [512, 768, 768], P(('groups', 'walk'), 'pairs', 'chol'), as said below
- trial_orbitals: float32 [768, 256], P('groups'), as said below
- walkers: float32 [16, 768, 256], P(('groups', 'pairs', 'chol'), None, 'walk'), as said below
- field_noise: float32 [1, 16, 512], P('groups', None, 'walk'), may hold values from -6 to 6
Outputs:
- propagated: float32 [16, 768, 256], P(('groups', 'pairs', 'chol'), None, 'walk')
- force_bias: float32 [1, 16, 512], P('groups', None, 'walk')
Inputs may be any that keep to these rules, and one draw needn't show every extreme that they name: chol_vectors[g, p, q] = chol_vectors[g, q, p] for every g. The columns of trial_orbitals are linearly independent. `walkers`: every walker's intersection with trial_orbitals is far from singular.
All inputs are finite; a program needn't handle non-finite values.
Results may differ from a plain program's by a relative error of at most 0.0029.
Values may be sent and summed in bfloat16 or wider, within the bound.
A program may use at most 64 MiB of HBM per device.

v0:
```python
import functools

import jax
import jax.numpy as jnp
from jax import lax
from jax.experimental import pallas as pl
from jax.experimental.pallas import tpu as pltpu
from jax.sharding import PartitionSpec as P

TERMS = 6


root_step = 0.05
highest = lax.Precision.HIGHEST


def swapped(value, axis, apart):
    mask = 2**apart
    pairs = [(source, source ^ mask) for source in range(lax.axis_size(axis))]
    return lax.ppermute(value, axis, pairs)


def solve_normal(factor, right_side):
    middle = lax.linalg.triangular_solve(factor, right_side, left_side=True, lower=True)
    return lax.linalg.triangular_solve(factor, middle, left_side=True, lower=True, transpose_a=True)


def green_blocks(walker_full, trial_orbitals, trial_part, row_groups, col_groups):
    owner_walkers, orbital_count, electron_count = walker_full.shape
    intersection = jnp.einsum("nm,wnk->wmk", trial_orbitals, walker_full, precision=highest)
    normal = jnp.einsum("wmk,wml->wkl", intersection, intersection, precision=highest)
    factor = jnp.linalg.cholesky(normal)
    rotated = jnp.einsum("wmk,cbm->wkcb", intersection, trial_part, precision=highest)
    chosen_cols = rotated.shape[2] * rotated.shape[3]
    solved = solve_normal(factor, rotated.reshape(owner_walkers, electron_count, chosen_cols))
    slab_rows = orbital_count // row_groups
    block_cols = chosen_cols // col_groups
    shaped = solved.reshape(owner_walkers, electron_count, col_groups, block_cols)
    walker_rows = walker_full.reshape(owner_walkers, row_groups, slab_rows, electron_count)
    blocks = jnp.einsum("wiak,wkcb->icwab", walker_rows, shaped, precision=highest)
    return blocks.astype(jnp.bfloat16).reshape(
        row_groups * col_groups, owner_walkers, slab_rows * block_cols
    )


def plain_shards(chol_vectors, trial_orbitals, walkers, field_noise):
    held_vectors, slab_rows, slab_cols = chol_vectors.shape
    owner_walkers = walkers.shape[0]
    orbital_count = walkers.shape[1]
    electron_count = trial_orbitals.shape[1]
    row_groups = lax.axis_size("pairs")
    col_groups = lax.axis_size("chol")
    core_count = lax.axis_size("walk")
    core_index = lax.axis_index("walk")
    core_cols = slab_cols // core_count
    owner_count = row_groups * col_groups
    walker_total = owner_count * owner_walkers
    flat_vectors = chol_vectors.reshape(held_vectors, slab_rows * slab_cols)
    trial_split = trial_orbitals.reshape(col_groups, core_count, core_cols, electron_count)
    trial_part = lax.dynamic_index_in_dim(trial_split, core_index, 1, keepdims=False)
    walker_full = lax.all_gather(walkers, "walk", axis=2, tiled=True)
    outgoing = green_blocks(walker_full, trial_orbitals, trial_part, row_groups, col_groups)
    sectioned = outgoing.reshape(row_groups, col_groups, owner_walkers, slab_rows * core_cols)
    arrived = lax.all_to_all(
        lax.all_to_all(sectioned, "pairs", split_axis=0, concat_axis=0, tiled=True),
        "chol",
        split_axis=1,
        concat_axis=1,
        tiled=True,
    )
    arrived = arrived.reshape(walker_total, slab_rows, core_cols)
    partial_bias = jnp.einsum(
        "wab,gab->wg",
        lax.all_gather(arrived, "walk", axis=2, tiled=True),
        chol_vectors,
        preferred_element_type=jnp.float32,
    )
    force_bias = lax.psum(partial_bias, ("pairs", "chol"))
    bias_steps = [force_bias]
    shifted = field_noise[0] + root_step * force_bias
    shifted_high = lax.optimization_barrier(shifted.astype(jnp.bfloat16))
    shifted_low = (shifted - shifted_high.astype(jnp.float32)).astype(jnp.bfloat16)
    stacked = jnp.stack([shifted_high, shifted_low])
    both_parts = lax.dot_general(
        stacked, flat_vectors, (((2,), (0,)), ((), ())), preferred_element_type=jnp.float32
    )
    potential = both_parts[0] + both_parts[1]
    blocks_out = potential.reshape(owner_count, owner_walkers, slab_rows * slab_cols)
    received = lax.all_to_all(
        blocks_out, ("pairs", "chol"), split_axis=0, concat_axis=0, tiled=True
    )
    partner = swapped(received, "walk", 0)
    summed = (received + partner).reshape(
        row_groups, col_groups, owner_walkers, slab_rows, core_count, core_cols
    )
    matrix = jnp.transpose(summed, (2, 0, 3, 1, 4, 5)).reshape(
        owner_walkers, orbital_count, orbital_count
    )
    running_term = walkers
    running_sum = walkers
    for degree in range(1, TERMS):
        running_term = -(root_step / degree) * jnp.einsum(
            "wpq,wqm->wpm", matrix, running_term, precision=highest
        )
        running_sum = running_sum + running_term
    return (running_sum, jnp.stack(bias_steps))


PANEL = 32
TILE = 16
MIB = 2**20


def exact_dot(left, right, left_dim, right_dim):
    return lax.dot_general(
        left,
        right,
        (((left_dim,), (right_dim,)), ((), ())),
        precision=highest,
        preferred_element_type=jnp.float32,
    )


def fast_dot(left, right, left_dim, right_dim):
    return lax.dot_general(
        left, right, (((left_dim,), (right_dim,)), ((), ())), preferred_element_type=jnp.float32
    )


def green_kernel(row_groups, col_groups, walker_ref, trial_ref, out_ref, work):
    orbitals, electrons = walker_ref.shape
    core = lax.axis_index("walk")
    cores = lax.axis_size("walk")
    slab_rows = orbitals // row_groups
    slab_cols = orbitals // col_groups
    core_rows = slab_rows // cores
    half = core_rows // 2
    intersection = exact_dot(trial_ref[...], walker_ref[...], 0, 0)
    work[...] = exact_dot(intersection, intersection, 0, 0)
    lanes = lax.broadcasted_iota(jnp.int32, (PANEL, electrons), 1)
    rows = lax.broadcasted_iota(jnp.int32, (PANEL, electrons), 0)
    wide = lax.broadcasted_iota(jnp.int32, (electrons, electrons), 1)
    for start in range(0, electrons, PANEL):
        panel = work[start : start + PANEL, :]
        signed = jnp.where(lanes < start, -panel, panel)
        for step in range(PANEL):
            lane = start + step
            pivot_col = panel[:, lane : lane + 1]
            pivot = panel[step : step + 1, lane : lane + 1]
            scaled = jnp.where(lanes[:1] == lane, 1.0, panel[step : step + 1, :]) * (1.0 / pivot)
            cleared = jnp.where(lanes == lane, 0.0, panel) - pivot_col * scaled
            panel = jnp.where(rows == step, scaled, cleared)
        update = exact_dot(signed, panel, 0, 0)
        inside = (wide >= start) & (wide < start + PANEL)
        work[...] = jnp.where(inside, 0.0, work[...]) - update
        work[start : start + PANEL, :] = panel
    inverse = exact_dot(work[...], intersection, 1, 1)
    identity = jnp.where(
        lax.broadcasted_iota(jnp.int32, (electrons, electrons), 0) == wide, 1.0, 0.0
    )
    rest = identity - exact_dot(intersection, inverse, 1, 0)
    inverse = inverse + exact_dot(inverse, rest, 1, 0)
    chosen = jnp.concatenate(
        [
            walker_ref[pl.ds(pl.multiple_of(row * slab_rows + core * core_rows, 8), core_rows), :]
            for row in range(row_groups)
        ],
        axis=0,
    )
    left = exact_dot(chosen, inverse, 1, 0)
    for col in range(col_groups):
        block = exact_dot(left, trial_ref[col * slab_cols : (col + 1) * slab_cols, :], 1, 1)
        for row in range(row_groups):
            top = block[row * core_rows : row * core_rows + half]
            low = block[row * core_rows + half : (row + 1) * core_rows]
            out_ref[row * col_groups + col] = jnp.concatenate([top, low], axis=1).astype(jnp.bfloat16)


def walk_kernel(
    row_groups,
    col_groups,
    green_ref,
    vectors_ref,
    walker_ref,
    noise_ref,
    out_ref,
    bias_ref,
    held,
    greens,
    tiles,
    traces,
    first_sums,
    second_sums,
    spread,
    partner,
    own,
    ready,
    arrived,
    matrix,
    load_sem,
    green_send,
    green_recv,
    pass_send,
    pass_recv,
    first_send,
    first_recv,
    second_send,
    second_recv,
    partner_send,
    partner_recv,
    out_send,
    out_recv,
    hand_send,
    hand_recv,
):
    owners = row_groups * col_groups
    window, slab_rows, slab_cols = held.shape
    half = green_ref.shape[1]
    pieces = half // TILE
    blocks = slab_rows // TILE
    pair = lax.axis_index("pairs")
    place = lax.axis_index("chol")
    core = lax.axis_index("walk")
    me = pair * col_groups + place
    other = {"walk": 1 - core}

    def chip(index):
        return {"pairs": index // col_groups, "chol": index % col_groups}

    def to(shift):
        return lax.rem(me + shift, owners)

    def source(shift):
        return lax.rem(me + owners - shift, owners)

    def remote(src, dst, send, recv, target):
        return pltpu.make_async_remote_copy(
            src_ref=src,
            dst_ref=dst,
            send_sem=send,
            recv_sem=recv,
            device_id=target,
            device_id_type=pl.DeviceIdType.MESH,
        )

    parts = load_sem.shape[0]
    depth = window // parts
    loads = [
        pltpu.make_async_copy(
            vectors_ref.at[pl.ds(index * depth, depth)],
            held.at[pl.ds(index * depth, depth)],
            load_sem.at[index],
        )
        for index in range(parts)
    ]
    barrier = pltpu.get_barrier_semaphore()
    for shift in range(1, owners):
        pl.semaphore_signal(barrier, inc=1, device_id=chip(to(shift)), device_id_type=pl.DeviceIdType.MESH)
    pl.semaphore_signal(barrier, inc=1, device_id=other, device_id_type=pl.DeviceIdType.MESH)
    pl.semaphore_wait(barrier, owners)

    def green_copy(shift, slot):
        return remote(
            green_ref.at[to(shift)], greens.at[core, slot], green_send.at[shift],
            green_recv.at[shift], chip(to(shift)),
        )

    def pass_copy(shift, side):
        slot = source(shift)
        return remote(
            greens.at[side, slot], greens.at[side, slot], pass_send.at[shift], pass_recv.at[shift], other
        )

    for shift in range(1, owners):
        green_copy(shift, me).start()
    for load in loads:
        load.start()
    greens[core, me] = green_ref[me]
    pass_copy(0, core).start()
    for shift in range(1, owners):
        green_copy(shift, source(shift)).wait_recv()
        pass_copy(shift, core).start()
    for shift in range(1, owners):
        green_copy(shift, me).wait_send()
    for shift in range(owners):
        pass_copy(shift, 1 - core).wait_recv()
    for shift in range(owners):
        pass_copy(shift, core).wait_send()
    width = 2 * slab_cols
    for side in range(2):
        for piece in range(pieces):
            both = greens[side, :, piece * TILE : (piece + 1) * TILE, :].reshape(owners * TILE, width)
            tiles[side * 2 * pieces + piece] = both[:, :slab_cols]
            turned = pltpu.roll(both.astype(jnp.float32), slab_cols, 1)
            tiles[side * 2 * pieces + pieces + piece] = turned[:, :slab_cols].astype(jnp.bfloat16)
    for load in loads:
        load.wait()

    batch = min(window, 32)
    same = lax.rem(lax.broadcasted_iota(jnp.int32, (TILE, owners * TILE), 1), TILE) == (
        lax.broadcasted_iota(jnp.int32, (TILE, owners * TILE), 0)
    )

    @pl.loop(0, window // batch)
    def _(index):
        begin = pl.multiple_of(index * batch, batch)
        total = jnp.zeros((batch * TILE, owners * TILE), jnp.float32)
        for block in range(blocks):
            left = held[pl.ds(begin, batch), block * TILE : (block + 1) * TILE, :]
            total += fast_dot(left.reshape(batch * TILE, slab_cols), tiles[block], 1, 1)
        kept = jnp.where(same[None], total.reshape(batch, TILE, owners * TILE), 0.0)
        traces[pl.ds(begin, batch), :] = jnp.sum(kept, axis=1)

    walker_row = lax.broadcasted_iota(jnp.int32, (owners, owners * TILE), 0)
    column = lax.broadcasted_iota(jnp.int32, (owners, owners * TILE), 1)
    picker = jnp.where(walker_row == column // TILE, 1.0, 0.0)
    first_sums[place] = exact_dot(picker, traces[...], 1, 1)

    def first_copy(shift, slot):
        target = lax.rem(place + shift, col_groups)
        return remote(
            first_sums.at[slot], first_sums.at[slot], first_send.at[shift], first_recv.at[shift], {"chol": target}
        )

    def second_copy(shift, slot):
        target = lax.rem(pair + shift, row_groups)
        return remote(
            second_sums.at[slot], second_sums.at[slot], second_send.at[shift], second_recv.at[shift], {"pairs": target}
        )

    for shift in range(1, col_groups):
        first_copy(shift, place).start()
    for shift in range(1, col_groups):
        first_copy(shift, lax.rem(place + col_groups - shift, col_groups)).wait_recv()
    summed = first_sums[0]
    for slot in range(1, col_groups):
        summed = summed + first_sums[slot]
    second_sums[pair] = summed
    for shift in range(1, row_groups):
        second_copy(shift, pair).start()
    for shift in range(1, row_groups):
        second_copy(shift, lax.rem(pair + row_groups - shift, row_groups)).wait_recv()
    bias = second_sums[0]
    for slot in range(1, row_groups):
        bias = bias + second_sums[slot]
    bias_ref[0] = bias
    for shift in range(1, col_groups):
        first_copy(shift, place).wait_send()
    for shift in range(1, row_groups):
        second_copy(shift, pair).wait_send()

    shifted = (noise_ref[0] + root_step * bias).astype(jnp.bfloat16)
    tall = (owners * TILE, owners)
    repeat = jnp.where(
        lax.broadcasted_iota(jnp.int32, tall, 0) // TILE == lax.broadcasted_iota(jnp.int32, tall, 1), 1.0, 0.0
    ).astype(jnp.bfloat16)
    repeated = fast_dot(repeat, shifted, 1, 0).astype(jnp.bfloat16)
    group = 16
    spans = window // group
    square = (owners * TILE, group * TILE)
    diagonal = lax.rem(lax.broadcasted_iota(jnp.int32, square, 0), TILE) == lax.rem(
        lax.broadcasted_iota(jnp.int32, square, 1), TILE
    )
    for span in range(spans):
        shape = (window, group * TILE)
        opened = jnp.where(
            lax.broadcasted_iota(jnp.int32, shape, 0)
            == span * group + lax.broadcasted_iota(jnp.int32, shape, 1) // TILE,
            1.0,
            0.0,
        ).astype(jnp.bfloat16)
        wide = fast_dot(repeated, opened, 1, 0)
        spread[span] = jnp.where(diagonal, wide, 0.0).astype(jnp.bfloat16)

    def potential(block):
        row = pl.multiple_of(block * TILE, TILE)
        total = jnp.zeros((owners * TILE, slab_cols), jnp.float32)
        for span in range(spans):
            right = held[span * group : (span + 1) * group, pl.ds(row, TILE), :]
            total += fast_dot(spread[span], right.reshape(group * TILE, slab_cols), 1, 0)
        return total

    def packed(side, piece):
        first = side * 2 * pieces + piece
        both = jnp.concatenate([potential(first), potential(first + pieces)], axis=1)
        return both.reshape(owners, TILE, width)

    def partner_copy(piece):
        return remote(
            own.at[piece], partner.at[piece], partner_send.at[piece], partner_recv.at[piece], other
        )

    def out_copy(piece, shift, slot):
        span = pl.ds(piece * TILE, TILE)
        return remote(
            ready.at[to(shift), span], arrived.at[core, slot, span], out_send.at[piece, shift],
            out_recv.at[piece, shift], chip(to(shift)),
        )

    def hand_copy(shift, side):
        slot = source(shift)
        return remote(
            arrived.at[side, slot], arrived.at[side, slot], hand_send.at[shift], hand_recv.at[shift], other
        )

    for piece in range(pieces):
        own[piece] = packed(1 - core, piece)
        partner_copy(piece).start()
    for piece in range(pieces):
        mine = packed(core, piece)
        partner_copy(piece).wait_recv()
        ready[:, piece * TILE : (piece + 1) * TILE, :] = (mine + partner[piece]).astype(jnp.bfloat16)
        for shift in range(1, owners):
            out_copy(piece, shift, me).start()
    arrived[core, me] = ready[me]
    hand_copy(0, core).start()
    for shift in range(1, owners):
        for piece in range(pieces):
            out_copy(piece, shift, source(shift)).wait_recv()
        hand_copy(shift, core).start()
    for piece in range(pieces):
        partner_copy(piece).wait_send()
        for shift in range(1, owners):
            out_copy(piece, shift, me).wait_send()
    for shift in range(owners):
        hand_copy(shift, 1 - core).wait_recv()
    for shift in range(owners):
        hand_copy(shift, core).wait_send()
    for slot in range(owners):
        for side in range(2):
            base = (slot // col_groups) * slab_rows + side * 2 * half
            both = arrived[side, slot]
            matrix[slot % col_groups, base : base + half, :] = both[:, :slab_cols]
            turned = pltpu.roll(both.astype(jnp.float32), slab_cols, 1)
            matrix[slot % col_groups, base + half : base + 2 * half, :] = turned[:, :slab_cols].astype(jnp.bfloat16)

    term = walker_ref[0]
    out_ref[0] = term
    share = term.shape[1]
    for degree in range(1, TERMS):
        high = term.astype(jnp.bfloat16)
        low = (term - high.astype(jnp.float32)).astype(jnp.bfloat16)
        sides = jnp.concatenate([high, low], axis=1)
        total = jnp.zeros((term.shape[0], 2 * share), jnp.float32)
        for col in range(col_groups):
            total += fast_dot(matrix[col], sides[col * slab_cols : (col + 1) * slab_cols], 1, 0)
        term = -(root_step / degree) * (total[:, :share] + total[:, share:])
        out_ref[0] = out_ref[0] + term


def fits(chol_vectors, trial_orbitals, walkers):
    window, slab_rows, slab_cols = chol_vectors.shape
    electrons = trial_orbitals.shape[1]
    owners = lax.axis_size("pairs") * lax.axis_size("chol")
    return (
        lax.axis_size("walk") == 2
        and walkers.shape[0] == 1
        and walkers.shape[1] == trial_orbitals.shape[0]
        and slab_rows % (4 * TILE) == 0
        and (2 * slab_cols) % 128 == 0
        and window % 128 == 0
        and electrons % 256 == 0
        and owners <= 16
        and owners % 8 == 0
        and window * slab_rows * -(-slab_cols // 128) * 256 <= 28 * MIB
    )


def shards(chol_vectors, trial_orbitals, walkers, field_noise):
    if field_noise.shape[0] != 1 or not fits(chol_vectors, trial_orbitals, walkers):
        return plain_shards(chol_vectors, trial_orbitals, walkers, field_noise)
    row_groups = lax.axis_size("pairs")
    col_groups = lax.axis_size("chol")
    owners = row_groups * col_groups
    window, slab_rows, slab_cols = chol_vectors.shape
    orbitals, electrons = trial_orbitals.shape
    half = slab_rows // 4
    width = 2 * slab_cols
    pieces = half // TILE
    blocks = slab_rows // TILE
    walker_full = lax.all_gather(walkers[0], "walk", axis=1, tiled=True)
    in_vmem = pl.BlockSpec(memory_space=pltpu.VMEM)
    greens = pl.pallas_call(
        functools.partial(green_kernel, row_groups, col_groups),
        out_shape=jax.ShapeDtypeStruct((owners, half, width), jnp.bfloat16),
        in_specs=[in_vmem, in_vmem],
        out_specs=in_vmem,
        scratch_shapes=[pltpu.VMEM((electrons, electrons), jnp.float32)],
        compiler_params=pltpu.CompilerParams(vmem_limit_bytes=32 * MIB),
    )(walker_full, trial_orbitals)
    dma = pltpu.SemaphoreType.DMA
    propagated, bias = pl.pallas_call(
        functools.partial(walk_kernel, row_groups, col_groups),
        out_shape=(
            jax.ShapeDtypeStruct(walkers.shape, jnp.float32),
            jax.ShapeDtypeStruct(field_noise.shape, jnp.float32),
        ),
        in_specs=[in_vmem, pl.BlockSpec(memory_space=pl.ANY), in_vmem, in_vmem],
        out_specs=(in_vmem, in_vmem),
        scratch_shapes=[
            pltpu.VMEM(chol_vectors.shape, jnp.bfloat16),
            pltpu.VMEM((2, owners, half, width), jnp.bfloat16),
            pltpu.VMEM((blocks, owners * TILE, slab_cols), jnp.bfloat16),
            pltpu.VMEM((window, owners * TILE), jnp.float32),
            pltpu.VMEM((col_groups, owners, window), jnp.float32),
            pltpu.VMEM((row_groups, owners, window), jnp.float32),
            pltpu.VMEM((window // 16, owners * TILE, 16 * TILE), jnp.bfloat16),
            pltpu.VMEM((pieces, owners, TILE, width), jnp.float32),
            pltpu.VMEM((pieces, owners, TILE, width), jnp.float32),
            pltpu.VMEM((owners, half, width), jnp.bfloat16),
            pltpu.VMEM((2, owners, half, width), jnp.bfloat16),
            pltpu.VMEM((col_groups, orbitals, slab_cols), jnp.bfloat16),
            dma((4,)),
            dma((owners,)),
            dma((owners,)),
            dma((owners,)),
            dma((owners,)),
            dma((col_groups,)),
            dma((col_groups,)),
            dma((row_groups,)),
            dma((row_groups,)),
            dma((pieces,)),
            dma((pieces,)),
            dma((pieces, owners)),
            dma((pieces, owners)),
            dma((owners,)),
            dma((owners,)),
        ],
        compiler_params=pltpu.CompilerParams(
            collective_id=0, has_side_effects=True, vmem_limit_bytes=56 * MIB
        ),
    )(greens, chol_vectors, walkers, field_noise)
    return (propagated, bias)


def solution(mesh):
    placed = (
        P(("groups", "walk"), "pairs", "chol"),
        P("groups", None),
        P(("groups", "pairs", "chol"), None, "walk"),
        P("groups", None, "walk"),
    )
    return jax.shard_map(
        shards,
        mesh=mesh,
        in_specs=placed,
        out_specs=(P(("groups", "pairs", "chol"), None, "walk"), P("groups", None, "walk")),
        check_vma=False,
    )
```

profile of v0, /device:TPU:0, one launch (start us, length us, event | category | flops | bytes accessed | tf_op | source)
XLA Modules:
  0.0 139.9 jit_solution(11095138024011600233)
XLA Ops:
  0.6 2.7 %all-gather = f32[1,768,256]{2,1,0:T(8,128)S(1)} all-gather(f32[1,768,128]{2,1,0:T(8,128)} %walker_ref.1), channel_id=2, replica_groups=mesh['groups'=1,'pairs'=4,'chol'=4,'walk'=2] {'walk'}, dimensions={2}, use_global_device_ids=true | all-gather | bytes 1179648 | tf_op jit(solution)/shard_map/all_gather | solution.py:481
  3.3 0.0 copy-start.1
  3.3 1.1 copy-done.1
  4.4 30.8 %shard_map.59.green_ref = bf16[16,48,384]{2,1,0:T(8,128)(2,1)S(1)} custom-call(f32[768,256]{1,0:T(8,128)S(1)} %bitcast.1, f32[768,256]{1,0:T(8,128)S(1)} %copy-done.1), custom_call_target="tpu_custom_call" | custom-call | tf_op jit(solution)/shard_map/pallas_call | solution.py:483
  35.2 0.0 copy-start
  35.2 0.9 copy-done
  36.1 34.1 %copy.6.vectors_ref = bf16[256,192,192]{2,1,0:T(8,128)(2,1)} copy(bf16[256,192,192]{0,2,1:T(8,128)(2,1)} %param.4) | data formatting | bytes 37748736 | tf_op args[0]
  70.2 66.6 %shard_map.60 = (f32[1,768,128]{2,1,0:T(8,128)}, f32[1,16,256]{2,1,0:T(8,128)}) custom-call(bf16[16,48,384]{2,1,0:T(8,128)(2,1)} %copy-done, bf16[256,192,192]{2,1,0:T(8,128)(2,1)} %copy.6.vectors_ref, f32[1,768,128]{2,1,0:T(8,128)} %walker_ref.1, f32[1,16,256]{2,1,0:T(8,128)} %noise_ref.1), custom_call_target="tpu_custom_call" | custom-call | tf_op jit(solution)/shard_map/pallas_call | solution.py:492
  136.8 1.8 %copy.9 = f32[1,768,128]{2,1,0:T(8,128)} copy(f32[1,768,128]{2,1,0:T(8,128)} %get-tuple-element.4) | data formatting | bytes 786432
  138.6 1.3 copy.10
Async XLA Ops:
  3.3 1.1 copy-start.1
  35.2 0.9 copy-start
where the time goes:
time: 141 us; the launch traced here: 140 us
  Pallas kernels  97.4 us (69%)
  local copies, waits for them, and re-layouts  39.2 us (28%)
  blocking collectives  2.66 us (2%)
    pallas_call x1, Pallas kernels, shards(): pl.pallas_call(functools.partial(walk_kernel, row_groups, col_groups), ou...  66.6 us
    unnamed x7, local copies, waits for them, and re-layouts  39.2 us
    pallas_call x1, Pallas kernels, shards(): pl.pallas_call(functools.partial(green_kernel, row_groups, col_groups), o...  30.8 us

commit v1 on v0

--- a/solution.py
+++ b/solution.py
@@ -143,13 +143,22 @@
     for start in range(0, electrons, PANEL):
         panel = work[start : start + PANEL, :]
         signed = jnp.where(lanes < start, -panel, panel)
-        for step in range(PANEL):
+        for step in range(0, PANEL, 2):
             lane = start + step
-            pivot_col = panel[:, lane : lane + 1]
-            pivot = panel[step : step + 1, lane : lane + 1]
-            scaled = jnp.where(lanes[:1] == lane, 1.0, panel[step : step + 1, :]) * (1.0 / pivot)
-            cleared = jnp.where(lanes == lane, 0.0, panel) - pivot_col * scaled
-            panel = jnp.where(rows == step, scaled, cleared)
+            left_col = panel[:, lane : lane + 1]
+            right_col = panel[:, lane + 1 : lane + 2]
+            a, b = left_col[step : step + 1], right_col[step : step + 1]
+            c, d = left_col[step + 1 : step + 2], right_col[step + 1 : step + 2]
+            scale = 1.0 / (a * d - b * c)
+            pivots = (lanes == lane) | (lanes == lane + 1)
+            unit_top = jnp.where(lanes[:1] == lane, 1.0, 0.0)
+            unit_low = jnp.where(lanes[:1] == lane + 1, 1.0, 0.0)
+            top = jnp.where(pivots[:1], unit_top, panel[step : step + 1, :])
+            low = jnp.where(pivots[:1], unit_low, panel[step + 1 : step + 2, :])
+            new_top = (d * scale) * top - (b * scale) * low
+            new_low = (a * scale) * low - (c * scale) * top
+            cleared = jnp.where(pivots, 0.0, panel) - left_col * new_top - right_col * new_low
+            panel = jnp.where(rows == step, new_top, jnp.where(rows == step + 1, new_low, cleared))
         update = exact_dot(signed, panel, 0, 0)
         inside = (wide >= start) & (wide < start + PANEL)
         work[...] = jnp.where(inside, 0.0, work[...]) - update
@@ -188,10 +197,9 @@
     held,
     greens,
     tiles,
-    traces,
+    sums,
     first_sums,
     second_sums,
-    spread,
     partner,
     own,
     ready,
@@ -214,10 +222,9 @@
     hand_recv,
 ):
     owners = row_groups * col_groups
-    window, slab_rows, slab_cols = held.shape
+    slab_rows, slab_cols, window = held.shape
     half = green_ref.shape[1]
     pieces = half // TILE
-    blocks = slab_rows // TILE
     pair = lax.axis_index("pairs")
     place = lax.axis_index("chol")
     core = lax.axis_index("walk")
@@ -244,7 +251,7 @@
         )
 
     parts = load_sem.shape[0]
-    depth = window // parts
+    depth = slab_rows // parts
     loads = [
         pltpu.make_async_copy(
             vectors_ref.at[pl.ds(index * depth, depth)],
@@ -289,32 +296,26 @@
     width = 2 * slab_cols
     for side in range(2):
         for piece in range(pieces):
-            both = greens[side, :, piece * TILE : (piece + 1) * TILE, :].reshape(owners * TILE, width)
-            tiles[side * 2 * pieces + piece] = both[:, :slab_cols]
-            turned = pltpu.roll(both.astype(jnp.float32), slab_cols, 1)
-            tiles[side * 2 * pieces + pieces + piece] = turned[:, :slab_cols].astype(jnp.bfloat16)
+            span = slice(piece * TILE, (piece + 1) * TILE)
+            both = jnp.swapaxes(greens[side, :, span, :].astype(jnp.float32), 0, 1)
+            row = side * 2 * half + piece * TILE
+            tiles[row : row + TILE] = both[:, :, :slab_cols].astype(jnp.bfloat16)
+            turned = pltpu.roll(both, slab_cols, 2)
+            tiles[row + half : row + half + TILE] = turned[:, :, :slab_cols].astype(jnp.bfloat16)
     for load in loads:
         load.wait()
 
-    batch = min(window, 32)
-    same = lax.rem(lax.broadcasted_iota(jnp.int32, (TILE, owners * TILE), 1), TILE) == (
-        lax.broadcasted_iota(jnp.int32, (TILE, owners * TILE), 0)
-    )
-
-    @pl.loop(0, window // batch)
+    sums[...] = jnp.zeros_like(sums)
+
+    @pl.loop(0, slab_rows // TILE)
     def _(index):
-        begin = pl.multiple_of(index * batch, batch)
-        total = jnp.zeros((batch * TILE, owners * TILE), jnp.float32)
-        for block in range(blocks):
-            left = held[pl.ds(begin, batch), block * TILE : (block + 1) * TILE, :]
-            total += fast_dot(left.reshape(batch * TILE, slab_cols), tiles[block], 1, 1)
-        kept = jnp.where(same[None], total.reshape(batch, TILE, owners * TILE), 0.0)
-        traces[pl.ds(begin, batch), :] = jnp.sum(kept, axis=1)
-
-    walker_row = lax.broadcasted_iota(jnp.int32, (owners, owners * TILE), 0)
-    column = lax.broadcasted_iota(jnp.int32, (owners, owners * TILE), 1)
-    picker = jnp.where(walker_row == column // TILE, 1.0, 0.0)
-    first_sums[place] = exact_dot(picker, traces[...], 1, 1)
+        total = sums[...]
+        for offset in range(TILE):
+            row = index * TILE + offset
+            total += fast_dot(tiles[row], held[row], 1, 0)
+        sums[...] = total
+
+    first_sums[place] = sums[...]
 
     def first_copy(shift, slot):
         target = lax.rem(place + shift, col_groups)
@@ -350,40 +351,15 @@
         second_copy(shift, pair).wait_send()
 
     shifted = (noise_ref[0] + root_step * bias).astype(jnp.bfloat16)
-    tall = (owners * TILE, owners)
-    repeat = jnp.where(
-        lax.broadcasted_iota(jnp.int32, tall, 0) // TILE == lax.broadcasted_iota(jnp.int32, tall, 1), 1.0, 0.0
-    ).astype(jnp.bfloat16)
-    repeated = fast_dot(repeat, shifted, 1, 0).astype(jnp.bfloat16)
-    group = 16
-    spans = window // group
-    square = (owners * TILE, group * TILE)
-    diagonal = lax.rem(lax.broadcasted_iota(jnp.int32, square, 0), TILE) == lax.rem(
-        lax.broadcasted_iota(jnp.int32, square, 1), TILE
-    )
-    for span in range(spans):
-        shape = (window, group * TILE)
-        opened = jnp.where(
-            lax.broadcasted_iota(jnp.int32, shape, 0)
-            == span * group + lax.broadcasted_iota(jnp.int32, shape, 1) // TILE,
-            1.0,
-            0.0,
-        ).astype(jnp.bfloat16)
-        wide = fast_dot(repeated, opened, 1, 0)
-        spread[span] = jnp.where(diagonal, wide, 0.0).astype(jnp.bfloat16)
 
     def potential(block):
-        row = pl.multiple_of(block * TILE, TILE)
-        total = jnp.zeros((owners * TILE, slab_cols), jnp.float32)
-        for span in range(spans):
-            right = held[span * group : (span + 1) * group, pl.ds(row, TILE), :]
-            total += fast_dot(spread[span], right.reshape(group * TILE, slab_cols), 1, 0)
-        return total
+        first = block * TILE
+        lines = [fast_dot(shifted, held[first + offset], 1, 1) for offset in range(TILE)]
+        return jnp.swapaxes(jnp.stack(lines), 0, 1)
 
     def packed(side, piece):
         first = side * 2 * pieces + piece
-        both = jnp.concatenate([potential(first), potential(first + pieces)], axis=1)
-        return both.reshape(owners, TILE, width)
+        return jnp.concatenate([potential(first), potential(first + pieces)], axis=2)
 
     def partner_copy(piece):
         return remote(
@@ -460,9 +436,8 @@
         and (2 * slab_cols) % 128 == 0
         and window % 128 == 0
         and electrons % 256 == 0
-        and owners <= 16
-        and owners % 8 == 0
-        and window * slab_rows * -(-slab_cols // 128) * 256 <= 28 * MIB
+        and owners == TILE
+        and chol_vectors.size <= 14 * MIB
     )
 
 
@@ -473,11 +448,11 @@
     col_groups = lax.axis_size("chol")
     owners = row_groups * col_groups
     window, slab_rows, slab_cols = chol_vectors.shape
+    vectors_last = jnp.transpose(chol_vectors, (1, 2, 0))
     orbitals, electrons = trial_orbitals.shape
     half = slab_rows // 4
     width = 2 * slab_cols
     pieces = half // TILE
-    blocks = slab_rows // TILE
     walker_full = lax.all_gather(walkers[0], "walk", axis=1, tiled=True)
     in_vmem = pl.BlockSpec(memory_space=pltpu.VMEM)
     greens = pl.pallas_call(
@@ -498,13 +473,12 @@
         in_specs=[in_vmem, pl.BlockSpec(memory_space=pl.ANY), in_vmem, in_vmem],
         out_specs=(in_vmem, in_vmem),
         scratch_shapes=[
-            pltpu.VMEM(chol_vectors.shape, jnp.bfloat16),
+            pltpu.VMEM(vectors_last.shape, jnp.bfloat16),
             pltpu.VMEM((2, owners, half, width), jnp.bfloat16),
-            pltpu.VMEM((blocks, owners * TILE, slab_cols), jnp.bfloat16),
-            pltpu.VMEM((window, owners * TILE), jnp.float32),
+            pltpu.VMEM((slab_rows, owners, slab_cols), jnp.bfloat16),
+            pltpu.VMEM((owners, window), jnp.float32),
             pltpu.VMEM((col_groups, owners, window), jnp.float32),
             pltpu.VMEM((row_groups, owners, window), jnp.float32),
-            pltpu.VMEM((window // 16, owners * TILE, 16 * TILE), jnp.bfloat16),
             pltpu.VMEM((pieces, owners, TILE, width), jnp.float32),
             pltpu.VMEM((pieces, owners, TILE, width), jnp.float32),
             pltpu.VMEM((owners, half, width), jnp.bfloat16),
@@ -529,7 +503,7 @@
         compiler_params=pltpu.CompilerParams(
             collective_id=0, has_side_effects=True, vmem_limit_bytes=56 * MIB
         ),
-    )(greens, chol_vectors, walkers, field_noise)
+    )(greens, vectors_last, walkers, field_noise)
     return (propagated, bias)
 
 

time: 141 us -> 116 us (0.82)
  local copies, waits for them, and re-layouts: 39.2 us -> 5.03 us
  Pallas kernels: 97.4 us -> 107 us
    unnamed x7 -> x6, local copies, waits for them, and re-layouts: 39.2 us -> 5.03 us
    pallas_call x1, Pallas kernels: 30.8 us -> 46.9 us  [shards(): pl.pallas_call(functools.partial(green_kernel, row_groups, col_groups), o...]
    pallas_call x1, Pallas kernels: 66.6 us -> 60.1 us  [shards(): pl.pallas_call(functools.partial(walk_kernel, row_groups, col_groups), ou...]
where the time goes in v1:
time: 116 us; the launch traced here: 115 us
  Pallas kernels  107 us (92%)
  local copies, waits for them, and re-layouts  5.03 us (4%)
  blocking collectives  2.66 us (2%)
    pallas_call x1, Pallas kernels, shards(): pl.pallas_call(functools.partial(walk_kernel, row_groups, col_groups), ou...  60.1 us
    pallas_call x1, Pallas kernels, shards(): pl.pallas_call(functools.partial(green_kernel, row_groups, col_groups), o...  46.9 us
    unnamed x6, local copies, waits for them, and re-layouts  5.03 us
    all_gather x1, blocking collectives, shards(): walker_full = lax.all_gather(walkers[0], 'walk', axis=1, tiled=True)  2.66 us

profile of v1, /device:TPU:0, one launch (start us, length us, event | category | flops | bytes accessed | tf_op | source)
XLA Modules:
  0.0 115.3 jit_solution(4693193650558206205)
XLA Ops:
  0.6 2.7 %all-gather = f32[1,768,256]{2,1,0:T(8,128)S(1)} all-gather(f32[1,768,128]{2,1,0:T(8,128)} %walker_ref.1), channel_id=2, replica_groups=mesh['groups'=1,'pairs'=4,'chol'=4,'walk'=2] {'walk'}, dimensions={2}, use_global_device_ids=true | all-gather | bytes 1179648 | tf_op jit(solution)/shard_map/all_gather | solution.py:456
  3.3 0.0 copy-start.1
  3.3 1.1 copy-done.1
  4.4 46.9 %shard_map.59.green_ref = bf16[16,48,384]{2,1,0:T(8,128)(2,1)S(1)} custom-call(f32[768,256]{1,0:T(8,128)S(1)} %bitcast.2, f32[768,256]{1,0:T(8,128)S(1)} %copy-done.1), custom_call_target="tpu_custom_call" | custom-call | tf_op jit(solution)/shard_map/pallas_call | solution.py:458
  51.4 0.0 copy-start
  51.4 0.8 copy-done
  52.2 60.1 %shard_map.60 = (f32[1,768,128]{2,1,0:T(8,128)}, f32[1,16,256]{2,1,0:T(8,128)}) custom-call(bf16[16,48,384]{2,1,0:T(8,128)(2,1)} %copy-done, bf16[192,192,256]{2,1,0:T(8,128)(2,1)} %bitcast.3, f32[1,768,128]{2,1,0:T(8,128)} %walker_ref.1, f32[1,16,256]{2,1,0:T(8,128)} %noise_ref.1), custom_call_target="tpu_custom_call" | custom-call | tf_op jit(solution)/shard_map/pallas_call | solution.py:467
  112.2 1.8 %copy.8 = f32[1,768,128]{2,1,0:T(8,128)} copy(f32[1,768,128]{2,1,0:T(8,128)} %get-tuple-element.4) | data formatting | bytes 786432
  114.0 1.3 %copy.9 = f32[1,16,256]{2,1,0:T(8,128)} copy(f32[1,16,256]{2,1,0:T(8,128)} %get-tuple-element.5) | data formatting | bytes 32768
Async XLA Ops:
  3.3 1.1 copy-start.1
  51.4 0.8 copy-start

commit v2 on v1

--- a/solution.py
+++ b/solution.py
@@ -143,22 +143,13 @@
     for start in range(0, electrons, PANEL):
         panel = work[start : start + PANEL, :]
         signed = jnp.where(lanes < start, -panel, panel)
-        for step in range(0, PANEL, 2):
+        for step in range(PANEL):
             lane = start + step
-            left_col = panel[:, lane : lane + 1]
-            right_col = panel[:, lane + 1 : lane + 2]
-            a, b = left_col[step : step + 1], right_col[step : step + 1]
-            c, d = left_col[step + 1 : step + 2], right_col[step + 1 : step + 2]
-            scale = 1.0 / (a * d - b * c)
-            pivots = (lanes == lane) | (lanes == lane + 1)
-            unit_top = jnp.where(lanes[:1] == lane, 1.0, 0.0)
-            unit_low = jnp.where(lanes[:1] == lane + 1, 1.0, 0.0)
-            top = jnp.where(pivots[:1], unit_top, panel[step : step + 1, :])
-            low = jnp.where(pivots[:1], unit_low, panel[step + 1 : step + 2, :])
-            new_top = (d * scale) * top - (b * scale) * low
-            new_low = (a * scale) * low - (c * scale) * top
-            cleared = jnp.where(pivots, 0.0, panel) - left_col * new_top - right_col * new_low
-            panel = jnp.where(rows == step, new_top, jnp.where(rows == step + 1, new_low, cleared))
+            pivot_col = panel[:, lane : lane + 1]
+            pivot = panel[step : step + 1, lane : lane + 1]
+            scaled = jnp.where(lanes[:1] == lane, 1.0, panel[step : step + 1, :]) * (1.0 / pivot)
+            cleared = jnp.where(lanes == lane, 0.0, panel) - pivot_col * scaled
+            panel = jnp.where(rows == step, scaled, cleared)
         update = exact_dot(signed, panel, 0, 0)
         inside = (wide >= start) & (wide < start + PANEL)
         work[...] = jnp.where(inside, 0.0, work[...]) - update

time: 116 us -> 99.6 us (0.86)
  Pallas kernels: 107 us -> 91 us
    pallas_call x1, Pallas kernels: 46.9 us -> 30.8 us  [shards(): pl.pallas_call(functools.partial(green_kernel, row_groups, col_groups), o...]
where the time goes in v2:
time: 99.6 us; the launch traced here: 99.3 us
  Pallas kernels  91 us (91%)
  local copies, waits for them, and re-layouts  5.03 us (5%)
  blocking collectives  2.66 us (3%)
    pallas_call x1, Pallas kernels, shards(): pl.pallas_call(functools.partial(walk_kernel, row_groups, col_groups), ou...  60.2 us
    pallas_call x1, Pallas kernels, shards(): pl.pallas_call(functools.partial(green_kernel, row_groups, col_groups), o...  30.8 us
    unnamed x6, local copies, waits for them, and re-layouts  5.03 us
    all_gather x1, blocking collectives, shards(): walker_full = lax.all_gather(walkers[0], 'walk', axis=1, tiled=True)  2.66 us

profile of v2, /device:TPU:0, one launch (start us, length us, event | category | flops | bytes accessed | tf_op | source)
XLA Modules:
  0.0 99.3 jit_solution(9788057381661737477)
XLA Ops:
  0.6 2.7 %all-gather = f32[1,768,256]{2,1,0:T(8,128)S(1)} all-gather(f32[1,768,128]{2,1,0:T(8,128)} %walker_ref.1), channel_id=2, replica_groups=mesh['groups'=1,'pairs'=4,'chol'=4,'walk'=2] {'walk'}, dimensions={2}, use_global_device_ids=true | all-gather | bytes 1179648 | tf_op jit(solution)/shard_map/all_gather | solution.py:447
  3.3 0.0 copy-start.1
  3.3 1.1 %copy-done.1 = f32[768,256]{1,0:T(8,128)S(1)} copy-done((f32[768,256]{1,0:T(8,128)S(1)}, f32[768,256]{1,0:T(8,128)}, u32[]{:S(2)}) %copy-start.1) | copy-done | bytes 786456
  4.4 30.8 %shard_map.59.green_ref = bf16[16,48,384]{2,1,0:T(8,128)(2,1)S(1)} custom-call(f32[768,256]{1,0:T(8,128)S(1)} %bitcast.2, f32[768,256]{1,0:T(8,128)S(1)} %copy-done.1), custom_call_target="tpu_custom_call" | custom-call | tf_op jit(solution)/shard_map/pallas_call | solution.py:449
  35.2 0.0 copy-start
  35.2 0.8 copy-done
  36.0 60.2 %shard_map.60 = (f32[1,768,128]{2,1,0:T(8,128)}, f32[1,16,256]{2,1,0:T(8,128)}) custom-call(bf16[16,48,384]{2,1,0:T(8,128)(2,1)} %copy-done, bf16[192,192,256]{2,1,0:T(8,128)(2,1)} %bitcast.3, f32[1,768,128]{2,1,0:T(8,128)} %walker_ref.1, f32[1,16,256]{2,1,0:T(8,128)} %noise_ref.1), custom_call_target="tpu_custom_call" | custom-call | tf_op jit(solution)/shard_map/pallas_call | solution.py:458
  96.2 1.8 %copy.8 = f32[1,768,128]{2,1,0:T(8,128)} copy(f32[1,768,128]{2,1,0:T(8,128)} %get-tuple-element.4) | data formatting | bytes 786432
  98.0 1.3 %copy.9 = f32[1,16,256]{2,1,0:T(8,128)} copy(f32[1,16,256]{2,1,0:T(8,128)} %get-tuple-element.5) | data formatting | bytes 32768
Async XLA Ops:
  3.3 1.1 %copy-start.1 = (f32[768,256]{1,0:T(8,128)S(1)}, f32[768,256]{1,0:T(8,128)}, u32[]{:S(2)}) copy-start(f32[768,256]{1,0:T(8,128)} %trial_ref.1) | copy-start | bytes 2359300
  35.2 0.8 copy-start
